TPU v7x, 256 devices: a whole 4x4x8 slice. The times are simulated.
256 devices in a mesh: row: 32 (over z, x), col: 8 (over y, core).
Axes of the slice: x: 4, y: 4, z: 8, core: 2. Of those that a mesh axis runs over, the one named last changes fastest.
Arguments:
- panel: float32 [128, 524288], P('col', 'row'), may hold values from -6 to 6
- signs: int32 [524288], P('row'), may hold values from -1 to 1, as said below
- offsets: int32 [32768], P('row'), may hold values from 0 to 16383
- owners: int32 [32768, 1], P('row'), may hold values from 0 to 31; in each aligned block of 1024 rows (0 to 1023, 1024 to 2047, ...) at most 64 rows name the same one
Outputs:
- grams: float32 [32, 128, 128], P('row', 'col')
Inputs may be any that keep to these rules, and one draw needn't show every extreme that they name: `signs`: each entry is +1 or -1. `owners`: in each aligned block of 1024 samples (the list of one source), no owner is named more than 64 times, a bound that some block reaches; every owner is named somewhere.
All inputs are finite; a program needn't handle non-finite values.
Results may differ from a plain program's by a relative error of at most 0.0003.
Values sent between devices are 32-bit elements; how exact they have to be, the bound alone decides.
A program may use at most 128 MiB of HBM per device.

v0:
```python
import jax
import jax.numpy as jnp
from jax import lax
from jax.sharding import PartitionSpec as P


def swapped(x, axis, distance):
    return lax.ppermute(x, axis, [(i, i ^ 1 << distance) for i in range(lax.axis_size(axis))])


def sylvester(order):
    index = jnp.arange(order, dtype=jnp.int32)
    common = jnp.bitwise_and(index[:, None], index[None, :])
    parity = jnp.zeros((order, order), jnp.int32)
    for level in range(max(order.bit_length() - 1, 0)):
        parity = parity + jnp.bitwise_and(jnp.right_shift(common, level), 1)
    return (1 - 2 * (parity % 2)).astype(jnp.float32)


def body(panel, signs, offsets, owners):
    col_width, row_count = panel.shape
    devices = lax.axis_size("row")
    blocks = row_count // 128
    sample_count = offsets.shape[0]
    high = lax.Precision.HIGHEST
    scale = 1.0 / jnp.sqrt(jnp.float32(devices * row_count))
    signed = (panel * signs.astype(jnp.float32)[None, :]).reshape(col_width, 128, blocks)
    inner = jnp.einsum("cab,bd->cad", signed, sylvester(blocks), precision=high)
    mixed = jnp.einsum("ea,cad->ced", sylvester(128), inner, precision=high)
    mixed = mixed.reshape(col_width, row_count) * scale
    my_index = lax.axis_index("row")
    for level in range(devices.bit_length() - 1):
        partner = swapped(mixed, "row", level)
        upper = jnp.bitwise_and(jnp.right_shift(my_index, level), 1) == 1
        mixed = jnp.where(upper, partner - mixed, mixed + partner)
    sampled = jnp.take(mixed, offsets, axis=1)
    full_rows = lax.all_gather(sampled, "col", axis=0, tiled=True)
    total_cols = full_rows.shape[0]
    owner_ids = owners[:, 0]
    capacity = 2 * sample_count // devices
    hits = (owner_ids[:, None] == jnp.arange(devices, dtype=jnp.int32)[None, :]).astype(jnp.int32)
    before = jnp.cumsum(hits, axis=0) - hits
    slot_index = jnp.sum(before * hits, axis=1)
    position = owner_ids * capacity + slot_index
    buffer = jnp.zeros((total_cols, devices * capacity), jnp.float32).at[:, position].set(full_rows)
    received = lax.all_to_all(
        buffer.reshape(total_cols, devices, capacity),
        "row",
        split_axis=1,
        concat_axis=1,
        tiled=True,
    )
    received = received.reshape(total_cols, devices * capacity)
    mine = lax.dynamic_slice_in_dim(received, lax.axis_index("col") * col_width, col_width, 0)
    gram = jnp.einsum("ck,dk->cd", mine, received, precision=high) / sample_count
    return gram[None]


def solution(mesh):
    placed = (P("col", "row"), P("row"), P("row"), P("row", None))
    return jax.shard_map(
        body, mesh=mesh, in_specs=placed, out_specs=P("row", "col", None), check_vma=False
    )
```

profile of v0, /device:TPU:2, one launch (start us, length us, event | category | flops | bytes accessed | tf_op | source)
XLA Modules:
  0.0 333.8 jit_solution(12955752235051832701)
XLA Ops:
  0.0 0.8 convert_element_type.18
  0.8 1.3 multiply_bitcast_fusion
  2.2 0.2 copy.35
  2.4 1.1 fusion.15
  3.5 1.0 fusion
  4.6 0.3 copy.14
  4.9 0.6 copy.39
  5.5 2.4 collective-permute-start
  7.9 4.6 %copy.16 = f32[16,16384]{0,1:T(8,128)} copy(f32[16,16384]{1,0:T(8,128)S(1)} %bitcast.46) | data formatting | bytes 2097152 | tf_op jit(solution)/shard_map/mul | solution.py:30
  12.5 18.0 %collective-permute-done = f32[16,16384]{1,0:T(8,128)S(1)} collective-permute-done((f32[16,16384]{1,0:T(8,128)S(1)}, f32[16,16384]{1,0:T(8,128)S(1)}, u32[]{:S(2)}, u32[]{:S(2)}) %collective-permute-start) | collective-permute-done | bytes 1048608 | tf_op jit(solution)/shard_map/ppermute | solution.py:8
  30.5 4.6 %copy.15 = f32[16,16384]{0,1:T(8,128)} copy(f32[16,16384]{1,0:T(8,128)S(1)} %collective-permute-done) | data formatting | bytes 2097152 | tf_op jit(solution)/shard_map/ppermute | solution.py:8
  35.1 9.8 %add_select_fusion.4 = f32[16,16384]{0,1:T(8,128)} fusion(f32[16,16384]{0,1:T(8,128)} %copy.16, f32[16,16384]{0,1:T(8,128)} %copy.15, pred[]{:T(512)S(6)} %eq.55), kind=kLoop, calls=%fused_computation.6 | loop fusion | flops 786432 | bytes 3145729 | tf_op jit(solution)/shard_map/jit(_where)/select_n | solution.py:35
  44.9 5.1 %copy.19 = f32[16,16384]{1,0:T(8,128)S(1)} copy(f32[16,16384]{0,1:T(8,128)} %add_select_fusion.4) | data formatting | bytes 2097152 | tf_op jit(solution)/shard_map/jit(_where)/select_n | solution.py:35
  50.0 2.2 collective-permute-start.1
  52.2 23.1 %collective-permute-done.1 = f32[16,16384]{1,0:T(8,128)S(1)} collective-permute-done((f32[16,16384]{1,0:T(8,128)S(1)}, f32[16,16384]{1,0:T(8,128)S(1)}, u32[]{:S(2)}, u32[]{:S(2)}) %collective-permute-start.1) | collective-permute-done | bytes 1048608 | tf_op jit(solution)/shard_map/ppermute | solution.py:8
  75.3 4.6 %copy.20 = f32[16,16384]{0,1:T(8,128)} copy(f32[16,16384]{1,0:T(8,128)S(1)} %collective-permute-done.1) | data formatting | bytes 2097152 | tf_op jit(solution)/shard_map/ppermute | solution.py:8
  79.9 9.8 %add_select_fusion.3 = f32[16,16384]{0,1:T(8,128)} fusion(f32[16,16384]{0,1:T(8,128)} %add_select_fusion.4, f32[16,16384]{0,1:T(8,128)} %copy.20, pred[]{:T(512)S(6)} %eq.54), kind=kLoop, calls=%fused_computation.5 | loop fusion | flops 786432 | bytes 3145729 | tf_op jit(solution)/shard_map/jit(_where)/select_n | solution.py:35
  89.7 5.1 %copy.22 = f32[16,16384]{1,0:T(8,128)S(1)} copy(f32[16,16384]{0,1:T(8,128)} %add_select_fusion.3) | data formatting | bytes 2097152 | tf_op jit(solution)/shard_map/jit(_where)/select_n | solution.py:35
  94.8 2.3 collective-permute-start.2
  97.1 21.4 %collective-permute-done.2 = f32[16,16384]{1,0:T(8,128)S(1)} collective-permute-done((f32[16,16384]{1,0:T(8,128)S(1)}, f32[16,16384]{1,0:T(8,128)S(1)}, u32[]{:S(2)}, u32[]{:S(2)}) %collective-permute-start.2) | collective-permute-done | bytes 1048608 | tf_op jit(solution)/shard_map/ppermute | solution.py:8
  118.5 4.6 %copy.23 = f32[16,16384]{0,1:T(8,128)} copy(f32[16,16384]{1,0:T(8,128)S(1)} %collective-permute-done.2) | data formatting | bytes 2097152 | tf_op jit(solution)/shard_map/ppermute | solution.py:8
  123.1 9.8 %add_select_fusion.2 = f32[16,16384]{0,1:T(8,128)} fusion(f32[16,16384]{0,1:T(8,128)} %add_select_fusion.3, f32[16,16384]{0,1:T(8,128)} %copy.23, pred[]{:T(512)S(6)} %eq.53), kind=kLoop, calls=%fused_computation.4 | loop fusion | flops 786432 | bytes 3145729 | tf_op jit(solution)/shard_map/jit(_where)/select_n | solution.py:35
  132.8 5.1 %copy.25 = f32[16,16384]{1,0:T(8,128)S(1)} copy(f32[16,16384]{0,1:T(8,128)} %add_select_fusion.2) | data formatting | bytes 2097152 | tf_op jit(solution)/shard_map/jit(_where)/select_n | solution.py:35
  137.9 3.3 %collective-permute-start.3 = (f32[16,16384]{1,0:T(8,128)S(1)}, f32[16,16384]{1,0:T(8,128)S(1)}, u32[]{:S(2)}, u32[]{:S(2)}) collective-permute-start(f32[16,16384]{1,0:T(8,128)S(1)} %copy.25), channel_id=1, source_target_pairs={{0,64},{8,72},{16,80},{24,88},{32,96},{40,104},{48,112},{56,120},{... | collective-permute-start | bytes 3145736 | tf_op jit(solution)/shard_map/ppermute | solution.py:8
  141.3 43.1 %collective-permute-done.3 = f32[16,16384]{1,0:T(8,128)S(1)} collective-permute-done((f32[16,16384]{1,0:T(8,128)S(1)}, f32[16,16384]{1,0:T(8,128)S(1)}, u32[]{:S(2)}, u32[]{:S(2)}) %collective-permute-start.3) | collective-permute-done | bytes 1048608 | tf_op jit(solution)/shard_map/ppermute | solution.py:8
  184.4 4.6 %copy.26 = f32[16,16384]{0,1:T(8,128)} copy(f32[16,16384]{1,0:T(8,128)S(1)} %collective-permute-done.3) | data formatting | bytes 2097152 | tf_op jit(solution)/shard_map/ppermute | solution.py:8
  189.0 9.8 %add_select_fusion.1 = f32[16,16384]{0,1:T(8,128)} fusion(f32[16,16384]{0,1:T(8,128)} %add_select_fusion.2, f32[16,16384]{0,1:T(8,128)} %copy.26, pred[]{:T(512)S(6)} %eq.52), kind=kLoop, calls=%fused_computation.3 | loop fusion | flops 786432 | bytes 3145729 | tf_op jit(solution)/shard_map/jit(_where)/select_n | solution.py:35
  198.7 0.0 copy-start
  198.7 0.0 copy-start.1
  198.7 5.1 %copy.28 = f32[16,16384]{1,0:T(8,128)S(1)} copy(f32[16,16384]{0,1:T(8,128)} %add_select_fusion.1) | data formatting | bytes 2097152 | tf_op jit(solution)/shard_map/jit(_where)/select_n | solution.py:35
  203.9 6.5 %collective-permute-start.4 = (f32[16,16384]{1,0:T(8,128)S(1)}, f32[16,16384]{1,0:T(8,128)S(1)}, u32[]{:S(2)}, u32[]{:S(2)}) collective-permute-start(f32[16,16384]{1,0:T(8,128)S(1)} %copy.28), channel_id=1, source_target_pairs={{0,128},{8,136},{16,144},{24,152},{32,160},{40,168},{48,176},{56,1... | collective-permute-start | bytes 3145736 | tf_op jit(solution)/shard_map/ppermute | solution.py:8
  210.4 0.0 copy-done
  210.4 9.0 %reduce-window.6 = s32[32,8,128]{2,1,0:T(8,128)S(1)} reduce-window(s32[32,8,128]{2,1,0:T(8,128)S(1)} %fusion.8, s32[]{:T(128)} %constant.29.clone.1), window={size=1x1x128 pad=0_0x0_0x127_0}, to_apply=%region_0.1 | reduce-window | flops 4161536 | bytes 262148 | tf_op jit(solution)/shard_map/reduce-window
  219.4 0.1 slice.10
  219.5 0.1 copy.11
  219.7 0.1 copy.12
  219.8 0.1 broadcast_add_fusion
  219.9 0.0 copy-done.1
  220.0 36.2 %collective-permute-done.4 = f32[16,16384]{1,0:T(8,128)S(1)} collective-permute-done((f32[16,16384]{1,0:T(8,128)S(1)}, f32[16,16384]{1,0:T(8,128)S(1)}, u32[]{:S(2)}, u32[]{:S(2)}) %collective-permute-start.4) | collective-permute-done | bytes 1048608 | tf_op jit(solution)/shard_map/ppermute | solution.py:8
  256.1 4.6 %copy.29 = f32[16,16384]{0,1:T(8,128)} copy(f32[16,16384]{1,0:T(8,128)S(1)} %collective-permute-done.4) | data formatting | bytes 2097152 | tf_op jit(solution)/shard_map/ppermute | solution.py:8
  260.7 9.8 %add_select_fusion = f32[16,16384]{0,1:T(8,128)} fusion(f32[16,16384]{0,1:T(8,128)} %add_select_fusion.1, f32[16,16384]{0,1:T(8,128)} %copy.29, pred[]{:T(512)S(6)} %eq.51), kind=kLoop, calls=%fused_computation.2 | loop fusion | flops 786432 | bytes 3145729 | tf_op jit(solution)/shard_map/jit(_where)/select_n | solution.py:35
  270.5 6.2 %gather_fusion = f32[1024,16]{1,0:T(8,128)S(1)} fusion(f32[16,16384]{0,1:T(8,128)} %add_select_fusion, s32[1024]{0:T(1024)S(1)} %fusion.31), kind=kCustom, calls=%fused_computation | custom fusion | bytes 135168 | tf_op jit(solution)/shard_map/jit(_take)/gather | solution.py:36
  276.7 0.2 select_bitcast_fusion
  276.9 0.2 copy.31
  277.1 13.6 %all_gather.3 = f32[128,1024]{1,0:T(8,128)S(1)} all-gather(f32[16,1024]{1,0:T(8,128)S(1)} %copy.31), channel_id=1, replica_groups=mesh['row'=32,'col'=8] {'col'}, dimensions={0}, use_global_device_ids=true | all-gather | bytes 589824 | tf_op jit(solution)/shard_map/all_gather | solution.py:37
  290.6 0.2 copy.32
  290.8 4.1 %scatter_custom_fusion = f32[128,2048]{0,1:T(8,128)} fusion(s32[1024]{0:T(1024)S(1)} %bitcast.56, f32[1024,128]{1,0:T(8,128)S(1)} %copy.32, f32[]{:T(128)} %constant.24.clone.1), kind=kCustom, calls=%fused_computation.15 | custom fusion | bytes 1048580 | tf_op jit(solution)/shard_map/scatter | solution.py:45
  294.9 7.5 %all-to-all-start = ((f32[128,32,64]{0,2,1:T(8,128)}), f32[128,32,64]{0,2,1:T(8,128)S(1)}, u32[]{:S(2)}, u32[]{:S(2)}) async-start(f32[128,32,64]{0,2,1:T(8,128)} %bitcast.10), calls=%async_computation | async-start | bytes 2097152 | tf_op jit(solution)/shard_map/all_to_all | solution.py:46
  302.5 28.6 %all-to-all-done = f32[128,32,64]{0,2,1:T(8,128)S(1)} async-done(((f32[128,32,64]{0,2,1:T(8,128)}), f32[128,32,64]{0,2,1:T(8,128)S(1)}, u32[]{:S(2)}, u32[]{:S(2)}) %all-to-all-start) | async-done | bytes 1048608 | tf_op jit(solution)/shard_map/all_to_all | solution.py:46
  331.0 2.8 fusion.1
  (7 shorter events, 0.1 us)
Async XLA Ops:
  5.5 25.0 %collective-permute-start = (f32[16,16384]{1,0:T(8,128)S(1)}, f32[16,16384]{1,0:T(8,128)S(1)}, u32[]{:S(2)}, u32[]{:S(2)}) collective-permute-start(f32[16,16384]{1,0:T(8,128)S(1)} %bitcast.45), channel_id=1, source_target_pairs={{0,8},{8,0},{16,24},{24,16},{32,40},{40,32},{48,56},{56,48},{64,72... | collective-permute-start | bytes 3145736 | tf_op jit(solution)/shard_map/ppermute | solution.py:8
  50.0 25.3 %collective-permute-start.1 = (f32[16,16384]{1,0:T(8,128)S(1)}, f32[16,16384]{1,0:T(8,128)S(1)}, u32[]{:S(2)}, u32[]{:S(2)}) collective-permute-start(f32[16,16384]{1,0:T(8,128)S(1)} %copy.19), channel_id=1, source_target_pairs={{0,16},{8,24},{16,0},{24,8},{32,48},{40,56},{48,32},{56,40},{64,80... | collective-permute-start | bytes 3145736 | tf_op jit(solution)/shard_map/ppermute | solution.py:8
  94.8 23.7 %collective-permute-start.2 = (f32[16,16384]{1,0:T(8,128)S(1)}, f32[16,16384]{1,0:T(8,128)S(1)}, u32[]{:S(2)}, u32[]{:S(2)}) collective-permute-start(f32[16,16384]{1,0:T(8,128)S(1)} %copy.22), channel_id=1, source_target_pairs={{0,32},{8,40},{16,48},{24,56},{32,0},{40,8},{48,16},{56,24},{64,96... | collective-permute-start | bytes 3145736 | tf_op jit(solution)/shard_map/ppermute | solution.py:8
  137.9 46.4 %collective-permute-start.3 = (f32[16,16384]{1,0:T(8,128)S(1)}, f32[16,16384]{1,0:T(8,128)S(1)}, u32[]{:S(2)}, u32[]{:S(2)}) collective-permute-start(f32[16,16384]{1,0:T(8,128)S(1)} %copy.25), channel_id=1, source_target_pairs={{0,64},{8,72},{16,80},{24,88},{32,96},{40,104},{48,112},{56,120},{... | collective-permute-start | bytes 3145736 | tf_op jit(solution)/shard_map/ppermute | solution.py:8
  198.7 11.6 %copy-start = (s32[1024,1]{0,1:T(1,128)S(1)}, s32[1024,1]{0,1:T(1,128)}, u32[]{:S(2)}) copy-start(s32[1024,1]{0,1:T(1,128)} %param.7) | copy-start | bytes 12292
  198.7 21.2 %copy-start.1 = (s32[1024]{0:T(1024)S(1)}, s32[1024]{0:T(1024)}, u32[]{:S(2)}) copy-start(s32[1024]{0:T(1024)} %param.6) | copy-start | bytes 12292
  203.9 52.3 %collective-permute-start.4 = (f32[16,16384]{1,0:T(8,128)S(1)}, f32[16,16384]{1,0:T(8,128)S(1)}, u32[]{:S(2)}, u32[]{:S(2)}) collective-permute-start(f32[16,16384]{1,0:T(8,128)S(1)} %copy.28), channel_id=1, source_target_pairs={{0,128},{8,136},{16,144},{24,152},{32,160},{40,168},{48,176},{56,1... | collective-permute-start | bytes 3145736 | tf_op jit(solution)/shard_map/ppermute | solution.py:8
  294.9 36.1 %all-to-all-start = ((f32[128,32,64]{0,2,1:T(8,128)}), f32[128,32,64]{0,2,1:T(8,128)S(1)}, u32[]{:S(2)}, u32[]{:S(2)}) async-start(f32[128,32,64]{0,2,1:T(8,128)} %bitcast.10), calls=%async_computation | async-start | bytes 2097152 | tf_op jit(solution)/shard_map/all_to_all | solution.py:46
where the time goes:
time: 334 us
  waiting for transfers between devices  170 us (51%)
  other arithmetic  60.4 us (18%)
  local copies, waits for them, and re-layouts  60.2 us (18%)
  starting transfers between devices  24.2 us (7%)
  blocking collectives  13.6 us (4%)
  matrix products  4.97 us (1%)
    ppermute x5, waiting for transfers between devices, swapped(): lax.ppermute(x, axis, [(i, i ^ 1 << distance) for i in range(lax.axis_siz...  142 us
    select_n x5, other arithmetic, body(): mixed = jnp.where(upper, partner - mixed, mixed + partner)  48.8 us
    all_to_all x1, waiting for transfers between devices, body(): lax.all_to_all(buffer.reshape(total_cols, devices, capacity), 'row', spli...  28.6 us
    ppermute x5, local copies, waits for them, and re-layouts, swapped(): lax.ppermute(x, axis, [(i, i ^ 1 << distance) for i in range(lax.axis_siz...  23 us
    select_n x4, local copies, waits for them, and re-layouts, body(): mixed = jnp.where(upper, partner - mixed, mixed + partner)  20.5 us
    ppermute x5, starting transfers between devices, swapped(): lax.ppermute(x, axis, [(i, i ^ 1 << distance) for i in range(lax.axis_siz...  16.7 us
    all_gather x1, blocking collectives, body(): full_rows = lax.all_gather(sampled, 'col', axis=0, tiled=True)  13.6 us
    another operation x3, other arithmetic  9.15 us
  transfers between devices with their start and end apart: 6, of which 6 were waited for; matrix products, arithmetic and copies ran while one was open for 4% of the time, Pallas kernels for 0%

commit v1 on v0

--- a/solution.py
+++ b/solution.py
@@ -34,7 +34,12 @@
         upper = jnp.bitwise_and(jnp.right_shift(my_index, level), 1) == 1
         mixed = jnp.where(upper, partner - mixed, mixed + partner)
     sampled = jnp.take(mixed, offsets, axis=1)
-    full_rows = lax.all_gather(sampled, "col", axis=0, tiled=True)
+    ring = [sampled]
+    for hop in range(7):
+        ring.append(lax.ppermute(ring[-1], "col", [(dev, (dev + 1) % 8) for dev in range(8)]))
+    full_rows = jnp.roll(
+        jnp.concatenate(ring[::-1], axis=0), (lax.axis_index("col") + 1) * ring[0].shape[0], axis=0
+    )
     total_cols = full_rows.shape[0]
     owner_ids = owners[:, 0]
     capacity = 2 * sample_count // devices

time: 334 us -> 389 us (1.16)
  waiting for transfers between devices: 170 us -> 231 us
  blocking collectives: 13.6 us -> 0 us
  local copies, waits for them, and re-layouts: 60.2 us -> 65.9 us
    ppermute x0 -> x7, waiting for transfers between devices: none -> 59.5 us  [body(): lax.ppermute(ring[-1], 'col', [(dev, (dev + 1) % 8) for dev in range(8)])]
    all_gather x1 -> x0, blocking collectives: 13.6 us -> none  [body(): full_rows = lax.all_gather(sampled, 'col', axis=0, tiled=True)]
    ppermute x5, waiting for transfers between devices: 142 us -> 151 us  [swapped(): lax.ppermute(x, axis, [(i, i ^ 1 << distance) for i in range(lax.axis_siz...]
    all_to_all x1, waiting for transfers between devices: 28.6 us -> 20.4 us  [body(): lax.all_to_all(buffer.reshape(total_cols, devices, capacity), 'row', spli...]
    concatenate x0 -> x1, local copies, waits for them, and re-layouts: none -> 5.73 us  [body(): jnp.roll(jnp.concatenate(ring[::-1], axis=0), (lax.axis_index('col') + 1)...]
  transfers between devices with their start and end apart: 6 -> 13, of which waited for: 6 -> 13; matrix products, arithmetic and copies ran while one was open for 4% -> 4% of each run, Pallas kernels for 0% -> 0%
where the time goes in v1:
time: 389 us; the launch traced here: 387 us
  waiting for transfers between devices  231 us (59%)
  local copies, waits for them, and re-layouts  65.9 us (17%)
  other arithmetic  60.3 us (16%)
  starting transfers between devices  24.2 us (6%)
  matrix products  4.97 us (1%)
    ppermute x5, waiting for transfers between devices, swapped(): lax.ppermute(x, axis, [(i, i ^ 1 << distance) for i in range(lax.axis_siz...  151 us
    ppermute x7, waiting for transfers between devices, body(): lax.ppermute(ring[-1], 'col', [(dev, (dev + 1) % 8) for dev in range(8)])  59.5 us
    select_n x5, other arithmetic, body(): mixed = jnp.where(upper, partner - mixed, mixed + partner)  48.7 us
    ppermute x5, local copies, waits for them, and re-layouts, swapped(): lax.ppermute(x, axis, [(i, i ^ 1 << distance) for i in range(lax.axis_siz...  23.1 us
    select_n x4, local copies, waits for them, and re-layouts, body(): mixed = jnp.where(upper, partner - mixed, mixed + partner)  20.4 us
    all_to_all x1, waiting for transfers between devices, body(): lax.all_to_all(buffer.reshape(total_cols, devices, capacity), 'row', spli...  20.4 us
    ppermute x5, starting transfers between devices, swapped(): lax.ppermute(x, axis, [(i, i ^ 1 << distance) for i in range(lax.axis_siz...  16.7 us
    another operation x3, other arithmetic  9.14 us
  transfers between devices with their start and end apart: 13, of which 13 were waited for; matrix products, arithmetic and copies ran while one was open for 4% of the time, Pallas kernels for 0%

profile of v1, /device:TPU:2, one launch (start us, length us, event | category | flops | bytes accessed | tf_op | source)
XLA Modules:
  0.0 386.7 jit_solution(452526835015450821)
XLA Ops:
  0.0 0.8 convert_element_type.18
  0.8 1.3 multiply_bitcast_fusion
  2.2 0.2 copy.33
  2.4 1.1 fusion.17
  3.5 1.0 fusion
  4.6 0.3 copy.14
  4.9 0.6 copy.37
  5.5 2.4 collective-permute-start
  7.9 4.6 %copy.16 = f32[16,16384]{0,1:T(8,128)} copy(f32[16,16384]{1,0:T(8,128)S(1)} %bitcast.48) | data formatting | bytes 2097152 | tf_op jit(solution)/shard_map/mul | solution.py:30
  12.5 18.1 %collective-permute-done = f32[16,16384]{1,0:T(8,128)S(1)} collective-permute-done((f32[16,16384]{1,0:T(8,128)S(1)}, f32[16,16384]{1,0:T(8,128)S(1)}, u32[]{:S(2)}, u32[]{:S(2)}) %collective-permute-start) | collective-permute-done | bytes 1048608 | tf_op jit(solution)/shard_map/ppermute | solution.py:8
  30.5 4.6 %copy.15 = f32[16,16384]{0,1:T(8,128)} copy(f32[16,16384]{1,0:T(8,128)S(1)} %collective-permute-done) | data formatting | bytes 2097152 | tf_op jit(solution)/shard_map/ppermute | solution.py:8
  35.1 9.7 %add_select_fusion.4 = f32[16,16384]{0,1:T(8,128)} fusion(f32[16,16384]{0,1:T(8,128)} %copy.16, f32[16,16384]{0,1:T(8,128)} %copy.15, pred[]{:T(512)S(6)} %eq.58), kind=kLoop, calls=%fused_computation.6 | loop fusion | flops 786432 | bytes 3145729 | tf_op jit(solution)/shard_map/jit(_where)/select_n | solution.py:35
  44.9 5.1 %copy.19 = f32[16,16384]{1,0:T(8,128)S(1)} copy(f32[16,16384]{0,1:T(8,128)} %add_select_fusion.4) | data formatting | bytes 2097152 | tf_op jit(solution)/shard_map/jit(_where)/select_n | solution.py:35
  50.0 2.2 collective-permute-start.1
  52.2 23.1 %collective-permute-done.1 = f32[16,16384]{1,0:T(8,128)S(1)} collective-permute-done((f32[16,16384]{1,0:T(8,128)S(1)}, f32[16,16384]{1,0:T(8,128)S(1)}, u32[]{:S(2)}, u32[]{:S(2)}) %collective-permute-start.1) | collective-permute-done | bytes 1048608 | tf_op jit(solution)/shard_map/ppermute | solution.py:8
  75.3 4.6 %copy.20 = f32[16,16384]{0,1:T(8,128)} copy(f32[16,16384]{1,0:T(8,128)S(1)} %collective-permute-done.1) | data formatting | bytes 2097152 | tf_op jit(solution)/shard_map/ppermute | solution.py:8
  79.9 9.7 %add_select_fusion.3 = f32[16,16384]{0,1:T(8,128)} fusion(f32[16,16384]{0,1:T(8,128)} %add_select_fusion.4, f32[16,16384]{0,1:T(8,128)} %copy.20, pred[]{:T(512)S(6)} %eq.57), kind=kLoop, calls=%fused_computation.5 | loop fusion | flops 786432 | bytes 3145729 | tf_op jit(solution)/shard_map/jit(_where)/select_n | solution.py:35
  89.7 5.1 %copy.22 = f32[16,16384]{1,0:T(8,128)S(1)} copy(f32[16,16384]{0,1:T(8,128)} %add_select_fusion.3) | data formatting | bytes 2097152 | tf_op jit(solution)/shard_map/jit(_where)/select_n | solution.py:35
  94.8 2.3 collective-permute-start.2
  97.1 21.4 %collective-permute-done.2 = f32[16,16384]{1,0:T(8,128)S(1)} collective-permute-done((f32[16,16384]{1,0:T(8,128)S(1)}, f32[16,16384]{1,0:T(8,128)S(1)}, u32[]{:S(2)}, u32[]{:S(2)}) %collective-permute-start.2) | collective-permute-done | bytes 1048608 | tf_op jit(solution)/shard_map/ppermute | solution.py:8
  118.5 4.6 %copy.23 = f32[16,16384]{0,1:T(8,128)} copy(f32[16,16384]{1,0:T(8,128)S(1)} %collective-permute-done.2) | data formatting | bytes 2097152 | tf_op jit(solution)/shard_map/ppermute | solution.py:8
  123.1 9.7 %add_select_fusion.2 = f32[16,16384]{0,1:T(8,128)} fusion(f32[16,16384]{0,1:T(8,128)} %add_select_fusion.3, f32[16,16384]{0,1:T(8,128)} %copy.23, pred[]{:T(512)S(6)} %eq.56), kind=kLoop, calls=%fused_computation.4 | loop fusion | flops 786432 | bytes 3145729 | tf_op jit(solution)/shard_map/jit(_where)/select_n | solution.py:35
  132.8 5.1 %copy.25 = f32[16,16384]{1,0:T(8,128)S(1)} copy(f32[16,16384]{0,1:T(8,128)} %add_select_fusion.2) | data formatting | bytes 2097152 | tf_op jit(solution)/shard_map/jit(_where)/select_n | solution.py:35
  137.9 3.3 collective-permute-start.3
  141.3 43.1 %collective-permute-done.3 = f32[16,16384]{1,0:T(8,128)S(1)} collective-permute-done((f32[16,16384]{1,0:T(8,128)S(1)}, f32[16,16384]{1,0:T(8,128)S(1)}, u32[]{:S(2)}, u32[]{:S(2)}) %collective-permute-start.3) | collective-permute-done | bytes 1048608 | tf_op jit(solution)/shard_map/ppermute | solution.py:8
  184.3 4.6 %copy.26 = f32[16,16384]{0,1:T(8,128)} copy(f32[16,16384]{1,0:T(8,128)S(1)} %collective-permute-done.3) | data formatting | bytes 2097152 | tf_op jit(solution)/shard_map/ppermute | solution.py:8
  189.0 9.7 %add_select_fusion.1 = f32[16,16384]{0,1:T(8,128)} fusion(f32[16,16384]{0,1:T(8,128)} %add_select_fusion.2, f32[16,16384]{0,1:T(8,128)} %copy.26, pred[]{:T(512)S(6)} %eq.55), kind=kLoop, calls=%fused_computation.3 | loop fusion | flops 786432 | bytes 3145729 | tf_op jit(solution)/shard_map/jit(_where)/select_n | solution.py:35
  198.7 0.0 copy-start.3
  198.7 5.1 %copy.28 = f32[16,16384]{1,0:T(8,128)S(1)} copy(f32[16,16384]{0,1:T(8,128)} %add_select_fusion.1) | data formatting | bytes 2097152 | tf_op jit(solution)/shard_map/jit(_where)/select_n | solution.py:35
  203.8 6.5 %collective-permute-start.4 = (f32[16,16384]{1,0:T(8,128)S(1)}, f32[16,16384]{1,0:T(8,128)S(1)}, u32[]{:S(2)}, u32[]{:S(2)}) collective-permute-start(f32[16,16384]{1,0:T(8,128)S(1)} %copy.28), channel_id=1, source_target_pairs={{0,128},{8,136},{16,144},{24,152},{32,160},{40,168},{48,176},{56,1... | collective-permute-start | bytes 3145736 | tf_op jit(solution)/shard_map/ppermute | solution.py:8
  210.3 0.0 copy-done.3
  210.4 45.7 %collective-permute-done.4 = f32[16,16384]{1,0:T(8,128)S(1)} collective-permute-done((f32[16,16384]{1,0:T(8,128)S(1)}, f32[16,16384]{1,0:T(8,128)S(1)}, u32[]{:S(2)}, u32[]{:S(2)}) %collective-permute-start.4) | collective-permute-done | bytes 1048608 | tf_op jit(solution)/shard_map/ppermute | solution.py:8
  256.1 4.6 %copy.29 = f32[16,16384]{0,1:T(8,128)} copy(f32[16,16384]{1,0:T(8,128)S(1)} %collective-permute-done.4) | data formatting | bytes 2097152 | tf_op jit(solution)/shard_map/ppermute | solution.py:8
  260.7 0.0 copy-start.2
  260.7 9.8 %add_select_fusion = f32[16,16384]{0,1:T(8,128)} fusion(f32[16,16384]{0,1:T(8,128)} %add_select_fusion.1, f32[16,16384]{0,1:T(8,128)} %copy.29, pred[]{:T(512)S(6)} %eq.54), kind=kLoop, calls=%fused_computation.2 | loop fusion | flops 786432 | bytes 3145729 | tf_op jit(solution)/shard_map/jit(_where)/select_n | solution.py:35
  270.5 6.2 %gather_fusion = f32[1024,16]{1,0:T(8,128)S(1)} fusion(f32[16,16384]{0,1:T(8,128)} %add_select_fusion, s32[1024]{0:T(1024)S(1)} %fusion.33), kind=kCustom, calls=%fused_computation | custom fusion | bytes 135168 | tf_op jit(solution)/shard_map/jit(_take)/gather | solution.py:36
  276.7 0.2 select_bitcast_fusion
  276.9 0.0 collective-permute-start.5
  276.9 9.8 %collective-permute-done.5 = f32[16,1024]{0,1:T(8,128)S(1)} collective-permute-done((f32[16,1024]{0,1:T(8,128)S(1)}, f32[16,1024]{0,1:T(8,128)S(1)}, u32[]{:S(2)}, u32[]{:S(2)}) %collective-permute-start.5) | collective-permute-done | bytes 65568 | tf_op jit(solution)/shard_map/ppermute | solution.py:39
  286.7 0.0 collective-permute-start.6
  286.7 9.8 %collective-permute-done.6 = f32[16,1024]{0,1:T(8,128)S(1)} collective-permute-done((f32[16,1024]{0,1:T(8,128)S(1)}, f32[16,1024]{0,1:T(8,128)S(1)}, u32[]{:S(2)}, u32[]{:S(2)}) %collective-permute-start.6) | collective-permute-done | bytes 65568 | tf_op jit(solution)/shard_map/ppermute | solution.py:39
  296.5 0.0 collective-permute-start.7
  296.5 9.8 %collective-permute-done.7 = f32[16,1024]{0,1:T(8,128)S(1)} collective-permute-done((f32[16,1024]{0,1:T(8,128)S(1)}, f32[16,1024]{0,1:T(8,128)S(1)}, u32[]{:S(2)}, u32[]{:S(2)}) %collective-permute-start.7) | collective-permute-done | bytes 65568 | tf_op jit(solution)/shard_map/ppermute | solution.py:39
  306.3 0.0 collective-permute-start.8
  306.3 0.0 copy-done.2
  306.4 9.0 %reduce-window.6 = s32[32,8,128]{2,1,0:T(8,128)S(1)} reduce-window(s32[32,8,128]{2,1,0:T(8,128)S(1)} %fusion.10, s32[]{:T(128)} %constant.77.clone.1), window={size=1x1x128 pad=0_0x0_0x127_0}, to_apply=%region_0.1 | reduce-window | flops 4161536 | bytes 262148 | tf_op jit(solution)/shard_map/reduce-window
  315.4 0.1 slice.10
  315.5 0.1 copy.11
  315.6 0.1 copy.12
  315.7 0.4 collective-permute-done.8
  316.2 0.0 collective-permute-start.9
  316.2 0.1 broadcast_add_fusion
  316.3 9.7 %collective-permute-done.9 = f32[16,1024]{0,1:T(8,128)S(1)} collective-permute-done((f32[16,1024]{0,1:T(8,128)S(1)}, f32[16,1024]{0,1:T(8,128)S(1)}, u32[]{:S(2)}, u32[]{:S(2)}) %collective-permute-start.9) | collective-permute-done | bytes 65568 | tf_op jit(solution)/shard_map/ppermute | solution.py:39
  326.0 0.0 collective-permute-start.10
  326.0 9.9 %collective-permute-done.10 = f32[16,1024]{0,1:T(8,128)} collective-permute-done((f32[16,1024]{0,1:T(8,128)S(1)}, f32[16,1024]{0,1:T(8,128)}, u32[]{:S(2)}, u32[]{:S(2)}) %collective-permute-start.10) | collective-permute-done | bytes 65568 | tf_op jit(solution)/shard_map/ppermute | solution.py:39
  335.9 0.0 collective-permute-start.11
  335.9 0.0 copy-done
  335.9 0.0 copy-done.1
  335.9 10.1 %collective-permute-done.11 = f32[16,1024]{0,1:T(8,128)} collective-permute-done((f32[16,1024]{0,1:T(8,128)}, f32[16,1024]{0,1:T(8,128)}, u32[]{:S(2)}, u32[]{:S(2)}) %collective-permute-start.11) | collective-permute-done | bytes 65568 | tf_op jit(solution)/shard_map/ppermute | solution.py:39
  346.0 5.7 %concatenate.6 = f32[256,1024]{0,1:T(8,128)S(1)} concatenate(f32[16,1024]{0,1:T(8,128)} %collective-permute-done.11, f32[16,1024]{0,1:T(8,128)} %collective-permute-done.10, f32[16,1024]{0,1:T(8,128)} %copy-done.1, f32[16,1024]{0,1:T(8,128)} %copy-done, f32[16,1024]{0,1:T(8,128)S(1)} %collective-permute-done.7, f32[16,1024]{0,1:T(8,128)S(1)} %collective-permute-done.6, ...), dimensions={0} | concatenate | bytes 2097152 | tf_op jit(solution)/shard_map/jit(_roll_dynamic)/concatenate | solution.py:40
  351.8 4.4 %scatter_custom_fusion = f32[128,2048]{0,1:T(8,128)} fusion(s32[1024]{0:T(1024)S(1)} %bitcast.57, f32[256,1024]{0,1:T(8,128)S(1)} %concatenate.6, s32[]{:T(128)S(6)} %select_n.86, s32[]{:T(128)} %constant.77.clone.1, f32[]{:T(128)} %constant.51.clone.1), kind=kCustom, calls=%fused_computation.14 | custom fusion | bytes 1572876 | tf_op jit(solution)/shard_map/scatter | solution.py:50
  356.1 7.5 %all-to-all-start = ((f32[128,32,64]{0,2,1:T(8,128)}), f32[128,32,64]{0,2,1:T(8,128)S(1)}, u32[]{:S(2)}, u32[]{:S(2)}) async-start(f32[128,32,64]{0,2,1:T(8,128)} %bitcast.10), calls=%async_computation | async-start | bytes 2097152 | tf_op jit(solution)/shard_map/all_to_all | solution.py:51
  363.6 20.4 %all-to-all-done = f32[128,32,64]{0,2,1:T(8,128)S(1)} async-done(((f32[128,32,64]{0,2,1:T(8,128)}), f32[128,32,64]{0,2,1:T(8,128)S(1)}, u32[]{:S(2)}, u32[]{:S(2)}) %all-to-all-start) | async-done | bytes 1048608 | tf_op jit(solution)/shard_map/all_to_all | solution.py:51
  384.0 2.8 fusion.1
  (9 shorter events, 0.1 us)
Async XLA Ops:
  5.5 25.0 %collective-permute-start = (f32[16,16384]{1,0:T(8,128)S(1)}, f32[16,16384]{1,0:T(8,128)S(1)}, u32[]{:S(2)}, u32[]{:S(2)}) collective-permute-start(f32[16,16384]{1,0:T(8,128)S(1)} %bitcast.47), channel_id=1, source_target_pairs={{0,8},{8,0},{16,24},{24,16},{32,40},{40,32},{48,56},{56,48},{64,72... | collective-permute-start | bytes 3145736 | tf_op jit(solution)/shard_map/ppermute | solution.py:8
  50.0 25.3 %collective-permute-start.1 = (f32[16,16384]{1,0:T(8,128)S(1)}, f32[16,16384]{1,0:T(8,128)S(1)}, u32[]{:S(2)}, u32[]{:S(2)}) collective-permute-start(f32[16,16384]{1,0:T(8,128)S(1)} %copy.19), channel_id=1, source_target_pairs={{0,16},{8,24},{16,0},{24,8},{32,48},{40,56},{48,32},{56,40},{64,80... | collective-permute-start | bytes 3145736 | tf_op jit(solution)/shard_map/ppermute | solution.py:8
  94.8 23.7 %collective-permute-start.2 = (f32[16,16384]{1,0:T(8,128)S(1)}, f32[16,16384]{1,0:T(8,128)S(1)}, u32[]{:S(2)}, u32[]{:S(2)}) collective-permute-start(f32[16,16384]{1,0:T(8,128)S(1)} %copy.22), channel_id=1, source_target_pairs={{0,32},{8,40},{16,48},{24,56},{32,0},{40,8},{48,16},{56,24},{64,96... | collective-permute-start | bytes 3145736 | tf_op jit(solution)/shard_map/ppermute | solution.py:8
  137.9 46.4 %collective-permute-start.3 = (f32[16,16384]{1,0:T(8,128)S(1)}, f32[16,16384]{1,0:T(8,128)S(1)}, u32[]{:S(2)}, u32[]{:S(2)}) collective-permute-start(f32[16,16384]{1,0:T(8,128)S(1)} %copy.25), channel_id=1, source_target_pairs={{0,64},{8,72},{16,80},{24,88},{32,96},{40,104},{48,112},{56,120},{... | collective-permute-start | bytes 3145736 | tf_op jit(solution)/shard_map/ppermute | solution.py:8
  198.7 11.6 %copy-start.3 = (s32[1024]{0:T(1024)S(1)}, s32[1024]{0:T(1024)}, u32[]{:S(2)}) copy-start(s32[1024]{0:T(1024)} %param.6) | copy-start | bytes 12292
  203.8 52.3 %collective-permute-start.4 = (f32[16,16384]{1,0:T(8,128)S(1)}, f32[16,16384]{1,0:T(8,128)S(1)}, u32[]{:S(2)}, u32[]{:S(2)}) collective-permute-start(f32[16,16384]{1,0:T(8,128)S(1)} %copy.28), channel_id=1, source_target_pairs={{0,128},{8,136},{16,144},{24,152},{32,160},{40,168},{48,176},{56,1... | collective-permute-start | bytes 3145736 | tf_op jit(solution)/shard_map/ppermute | solution.py:8
  260.7 45.6 %copy-start.2 = (s32[1024,1]{0,1:T(1,128)S(1)}, s32[1024,1]{0,1:T(1,128)}, u32[]{:S(2)}) copy-start(s32[1024,1]{0,1:T(1,128)} %param.7) | copy-start | bytes 12292
  276.9 9.8 %collective-permute-start.5 = (f32[16,1024]{0,1:T(8,128)S(1)}, f32[16,1024]{0,1:T(8,128)S(1)}, u32[]{:S(2)}, u32[]{:S(2)}) collective-permute-start(f32[16,1024]{0,1:T(8,128)S(1)} %select_bitcast_fusion), channel_id=1, source_target_pairs={{0,1},{1,2},{2,3},{3,4},{4,5},{5,6},{6,7},{7,0},{8,9},{9,10},{10,1... | collective-permute-start | bytes 196616 | tf_op jit(solution)/shard_map/ppermute | solution.py:39
  286.7 9.8 %collective-permute-start.6 = (f32[16,1024]{0,1:T(8,128)S(1)}, f32[16,1024]{0,1:T(8,128)S(1)}, u32[]{:S(2)}, u32[]{:S(2)}) collective-permute-start(f32[16,1024]{0,1:T(8,128)S(1)} %collective-permute-done.5), channel_id=1, source_target_pairs={{0,1},{1,2},{2,3},{3,4},{4,5},{5,6},{6,7},{7,0},{8,9},{9,10},{10,1... | collective-permute-start | bytes 196616 | tf_op jit(solution)/shard_map/ppermute | solution.py:39
  296.5 9.8 %collective-permute-start.7 = (f32[16,1024]{0,1:T(8,128)S(1)}, f32[16,1024]{0,1:T(8,128)S(1)}, u32[]{:S(2)}, u32[]{:S(2)}) collective-permute-start(f32[16,1024]{0,1:T(8,128)S(1)} %collective-permute-done.6), channel_id=1, source_target_pairs={{0,1},{1,2},{2,3},{3,4},{4,5},{5,6},{6,7},{7,0},{8,9},{9,10},{10,1... | collective-permute-start | bytes 196616 | tf_op jit(solution)/shard_map/ppermute | solution.py:39
  306.3 9.8 %collective-permute-start.8 = (f32[16,1024]{0,1:T(8,128)S(1)}, f32[16,1024]{0,1:T(8,128)S(1)}, u32[]{:S(2)}, u32[]{:S(2)}) collective-permute-start(f32[16,1024]{0,1:T(8,128)S(1)} %collective-permute-done.7), channel_id=1, source_target_pairs={{0,1},{1,2},{2,3},{3,4},{4,5},{5,6},{6,7},{7,0},{8,9},{9,10},{10,1... | collective-permute-start | bytes 196616 | tf_op jit(solution)/shard_map/ppermute | solution.py:39
  316.1 19.8 %copy-start = (f32[16,1024]{0,1:T(8,128)}, f32[16,1024]{0,1:T(8,128)S(1)}, u32[]{:S(2)}) copy-start(f32[16,1024]{0,1:T(8,128)S(1)} %collective-permute-done.8) | copy-start | bytes 196612
  316.2 9.8 %collective-permute-start.9 = (f32[16,1024]{0,1:T(8,128)S(1)}, f32[16,1024]{0,1:T(8,128)S(1)}, u32[]{:S(2)}, u32[]{:S(2)}) collective-permute-start(f32[16,1024]{0,1:T(8,128)S(1)} %collective-permute-done.8), channel_id=1, source_target_pairs={{0,1},{1,2},{2,3},{3,4},{4,5},{5,6},{6,7},{7,0},{8,9},{9,10},{10,1... | collective-permute-start | bytes 196616 | tf_op jit(solution)/shard_map/ppermute | solution.py:39
  326.0 10.0 %copy-start.1 = (f32[16,1024]{0,1:T(8,128)}, f32[16,1024]{0,1:T(8,128)S(1)}, u32[]{:S(2)}) copy-start(f32[16,1024]{0,1:T(8,128)S(1)} %collective-permute-done.9) | copy-start | bytes 196612
  326.0 9.9 %collective-permute-start.10 = (f32[16,1024]{0,1:T(8,128)S(1)}, f32[16,1024]{0,1:T(8,128)}, u32[]{:S(2)}, u32[]{:S(2)}) collective-permute-start(f32[16,1024]{0,1:T(8,128)S(1)} %collective-permute-done.9), channel_id=1, source_target_pairs={{0,1},{1,2},{2,3},{3,4},{4,5},{5,6},{6,7},{7,0},{8,9},{9,10},{10,1... | collective-permute-start | bytes 196616 | tf_op jit(solution)/shard_map/ppermute | solution.py:39
  335.9 10.1 %collective-permute-start.11 = (f32[16,1024]{0,1:T(8,128)}, f32[16,1024]{0,1:T(8,128)}, u32[]{:S(2)}, u32[]{:S(2)}) collective-permute-start(f32[16,1024]{0,1:T(8,128)} %collective-permute-done.10), channel_id=1, source_target_pairs={{0,1},{1,2},{2,3},{3,4},{4,5},{5,6},{6,7},{7,0},{8,9},{9,10},{10,1... | collective-permute-start | bytes 196616 | tf_op jit(solution)/shard_map/ppermute | solution.py:39
  356.1 27.8 %all-to-all-start = ((f32[128,32,64]{0,2,1:T(8,128)}), f32[128,32,64]{0,2,1:T(8,128)S(1)}, u32[]{:S(2)}, u32[]{:S(2)}) async-start(f32[128,32,64]{0,2,1:T(8,128)} %bitcast.10), calls=%async_computation | async-start | bytes 2097152 | tf_op jit(solution)/shard_map/all_to_all | solution.py:51
